TPU v7x, 32 devices: a whole 2x2x4 slice. The times are simulated.
32 devices in a mesh: group: 2 (over x), tile: 16 (over z, y, core).
Axes of the slice: x: 2, y: 2, z: 4, core: 2. Of those that a mesh axis runs over, the one named last changes fastest.
Arguments:
- samples: bfloat16 [2, 1024, 65984], P(None, ('group', 'tile')), parts along dimension 1, may hold values from -6 to 6
- fir_taps: float32 [8, 64], replicated, may hold values from -2 to 2
- chan_map: int32 [32], replicated, may hold values from 0 to 63, as said below
- layout: int32 [10], replicated, may hold values from 0 to 9, each once
Outputs:
- visibilities: float32 [640, 2, 128, 128], P(('group', 'tile')), parts along dimension 0
There are 2 independent parts, one for each index of `group`. A program takes and returns all parts, laid end to end along the dimension named above; an argument that names none is the same for every part. Nothing has to cross between parts.
Inputs may be any that keep to these rules, and one draw needn't show every extreme that they name: `chan_map`: 32 distinct channels in increasing order; channels 0 and 63 are always kept. `layout`: each block pair once.
All inputs are finite; a program needn't handle non-finite values.
Results may differ from a plain program's by a relative error of at most 0.0033.
Values may be sent and summed in bfloat16 or wider, within the bound.
A program may use at most 128 MiB of HBM per device.

v0:
```python
import math
import jax
import jax.numpy as jnp
import numpy as np
from jax import lax
from jax.sharding import PartitionSpec as P

NCHAN = 64
KEEP = 32
TAPS = 8
BLOCK = 128
CH = 4
NBLK = 4
NPAIR = 10


def swapped_2(block, axis, stride):
    count = lax.axis_size(axis)
    route = []
    for low in range(count):
        high = low | 1 << stride
        if high != low and high < count:
            route += [(low, high), (high, low)]
    return lax.ppermute(block, axis, route)


def pair_tables(block_count):
    first_block = []
    second_block = []
    for i in range(block_count):
        for j in range(i, block_count):
            first_block.append(i)
            second_block.append(j)
    return (np.array(first_block, np.int32), np.array(second_block, np.int32))


def dft_table(channels):
    tap_index = jnp.arange(NCHAN, dtype=jnp.int32).reshape((NCHAN,) + (1,) * channels.ndim)
    phases = tap_index * channels[None] % NCHAN
    angles = phases.astype(jnp.float32) * (2.0 * math.pi / NCHAN)
    scaling = 1.0 / math.sqrt(NCHAN)
    cosine = jnp.cos(angles) * scaling
    sine_part = jnp.sin(angles) * scaling
    real_rows = jnp.stack([cosine, -sine_part], 1)
    imag_rows = jnp.stack([sine_part, cosine], 1)
    return jnp.stack([real_rows, imag_rows], 0).astype(jnp.bfloat16)


def weigh(samples, fir_taps, spec_count):
    summed = jnp.zeros(samples.shape[:2] + (spec_count * NCHAN,), jnp.float32)
    for k in range(TAPS):
        window = lax.slice_in_dim(
            samples, k * NCHAN, k * NCHAN + spec_count * NCHAN, axis=2
        ).astype(jnp.float32)
        summed = summed + window * jnp.tile(fir_taps[k], spec_count)
    return summed.astype(jnp.bfloat16)


def lookup(positions, table_values):
    onehot = positions[:, None] == jnp.arange(table_values.shape[0], dtype=jnp.int32)[None, :]
    return jnp.sum(jnp.where(onehot, table_values[None, :], 0), 1).astype(jnp.int32)


def on_device(samples, fir_taps, chan_map, layout):
    tile_count = lax.axis_size("tile")
    in_dev = samples.shape[1]
    input_total = in_dev * tile_count
    spec_count = samples.shape[2] // NCHAN - TAPS + 1
    weighted = weigh(samples, fir_taps, spec_count)
    first_block, second_block = pair_tables(NBLK)
    first_table = jnp.asarray(first_block)
    second_table = jnp.asarray(second_block)
    tb_count = tile_count * CH // KEEP
    time_len = spec_count // tb_count
    first_sel = lookup(layout, first_table)
    second_sel = lookup(layout, second_table)
    dft_rows = dft_table(chan_map.reshape(KEEP // CH, CH))
    frames = weighted.reshape(2, in_dev, tb_count, time_len, NCHAN)
    spectra = jnp.einsum(
        "rnqoc,ribtn->obiqct", dft_rows, frames, preferred_element_type=jnp.float32
    )
    spectra = spectra.astype(jnp.bfloat16).reshape(tile_count, in_dev, 2, CH, time_len)
    received = lax.all_to_all(spectra, "tile", split_axis=0, concat_axis=1, tiled=True)
    c_items = received.shape[3]
    flat_inputs = received.reshape(input_total, 2, c_items, time_len)
    swapped = jnp.stack([-flat_inputs[:, 1], flat_inputs[:, 0]], 1)
    real_full = jnp.einsum(
        "apct,bpct->cab", flat_inputs, flat_inputs, preferred_element_type=jnp.float32
    )
    imag_full = jnp.einsum(
        "apct,bpct->cab", flat_inputs, swapped, preferred_element_type=jnp.float32
    )
    real_full = real_full.reshape(c_items, NBLK, BLOCK, NBLK, BLOCK)
    imag_full = imag_full.reshape(c_items, NBLK, BLOCK, NBLK, BLOCK)
    real_blocks = real_full[:, first_sel, :, second_sel, :]
    imag_blocks = imag_full[:, first_sel, :, second_sel, :]
    stacked = jnp.stack([real_blocks, imag_blocks], 2)
    partial_terms = jnp.swapaxes(stacked, 0, 1)
    row_terms = partial_terms.reshape(CH * NPAIR, 2, BLOCK, BLOCK)
    time_slot = lax.axis_index("tile") % tb_count
    level_count = tb_count.bit_length() - 1
    for bit_level in range(level_count - 1, -1, -1):
        half_rows = row_terms.shape[0] // 2
        upper_bit = time_slot // (1 << bit_level) % 2
        kept_rows = lax.dynamic_slice_in_dim(row_terms, upper_bit * half_rows, half_rows, 0)
        sent_rows = lax.dynamic_slice_in_dim(row_terms, (1 - upper_bit) * half_rows, half_rows, 0)
        row_terms = kept_rows + swapped_2(sent_rows, "tile", bit_level)
    return row_terms / spec_count


def solution(mesh):
    placed = (P(None, ("group", "tile"), None), P(), P(), P())
    return jax.shard_map(
        on_device,
        mesh=mesh,
        in_specs=placed,
        out_specs=P(("group", "tile"), None, None, None),
        check_vma=False,
    )
```

profile of v0, /device:TPU:17, one launch (start us, length us, event | category | flops | bytes accessed | tf_op | source)
XLA Modules:
  0.0 224.6 jit_solution(8689402433933781313)
XLA Ops:
  0.0 1.0 slice_bitcast_fusion.7
  2.5 34.4 %add_convert_fusion = bf16[2,32,65536]{2,1,0:T(8,128)(2,1)} fusion(f32[65536]{0:T(1024)S(1)} %mul.182, bf16[2,32,65984]{2,1,0:T(8,128)(2,1)} %param.6, f32[65536]{0:T(1024)S(1)} %mul.179, f32[65536]{0:T(1024)S(1)} %mul.176, f32[65536]{0:T(1024)S(1)} %mul.173, f32[65536]{0:T(1024)S(1)} %mul.170, f32[65536]{0:T(1024)S(1)} %mul.167, f32[65536]{0:T(1024)S(1)} %mul.164, ...), kind=kLoop, calls=%fused_computation.4 | loop fusion | flops 100663296 | bytes 77594624 | tf_op jit(solution)/shard_map/convert_element_type | solution.py:56
  36.9 18.2 %reshape.121 = bf16[2,32,2,512,64]{4,3,2,1,0:T(8,128)(2,1)} reshape(bf16[2,32,65536]{2,1,0:T(8,128)(2,1)} %add_convert_fusion) | data formatting | bytes 16777216 | tf_op jit(solution)/shard_map/reshape | solution.py:78
  55.4 10.9 %fusion.2 = bf16[8,2,32,2,4,512]{5,0,4,3,1,2:T(8,128)(2,1)S(1)} fusion(bf16[1,64,2,8,4]{1,3,0,4,2:T(8,128)(2,1)S(1)} %get-tuple-element.10, bf16[1,64,2,8,4]{1,3,0,4,2:T(8,128)(2,1)S(1)} %get-tuple-element.9, bf16[2,32,2,512,64]{4,3,2,1,0:T(8,128)(2,1)} %reshape.121), kind=kOutput, calls=%fused_computation.7 | convolution fusion | flops 539000832 | bytes 12599296 | tf_op jit(solution)/shard_map/rnqoc,ribtn->obiqct/dot_general | solution.py:79
  66.3 4.4 %copy.29 = bf16[8,2,32,2,4,512]{5,2,4,3,1,0:T(8,128)(2,1)} copy(bf16[8,2,32,2,4,512]{5,0,4,3,1,2:T(8,128)(2,1)S(1)} %fusion.2) | data formatting | bytes 8388608 | tf_op jit(solution)/shard_map/convert_element_type | solution.py:82
  70.7 6.6 %all-to-all-start = ((bf16[16,32,2,4,512]{4,1,3,2,0:T(8,128)(2,1)}), bf16[16,32,2,4,512]{4,1,3,2,0:T(8,128)(2,1)}, u32[]{:S(2)}, u32[]{:S(2)}) async-start(bf16[16,32,2,4,512]{4,1,3,2,0:T(8,128)(2,1)} %bitcast.66), calls=%async_computation | async-start | bytes 8388608 | tf_op jit(solution)/shard_map/all_to_all | solution.py:83
  77.5 92.0 %all-to-all-done = bf16[16,32,2,4,512]{4,1,3,2,0:T(8,128)(2,1)} async-done(((bf16[16,32,2,4,512]{4,1,3,2,0:T(8,128)(2,1)}), bf16[16,32,2,4,512]{4,1,3,2,0:T(8,128)(2,1)}, u32[]{:S(2)}, u32[]{:S(2)}) %all-to-all-start) | async-done | bytes 4194336 | tf_op jit(solution)/shard_map/all_to_all | solution.py:83
  169.5 2.5 %copy.30 = bf16[16,32,2,4,512]{4,1,0,2,3:T(8,128)(2,1)S(1)} copy(bf16[16,32,2,4,512]{4,1,3,2,0:T(8,128)(2,1)} %all-to-all-done) | data formatting | bytes 8388608 | tf_op jit(solution)/shard_map/all_to_all | solution.py:83
  172.0 0.3 slice_negate_fusion
  172.2 4.3 %convolution_bitcast_fusion = f32[4,512,512]{2,1,0:T(8,128)} fusion(bf16[512,2,4,512]{3,0,1,2:T(8,128)(2,1)S(1)} %bitcast.68), kind=kOutput, calls=%fused_computation.14 | convolution fusion | flops 2147483648 | bytes 8388608 | tf_op jit(solution)/shard_map/apct,bpct->cab/dot_general | solution.py:87
  176.6 4.4 %fusion.9 = f32[4,512,512]{2,1,0:T(8,128)} fusion(bf16[512,2,4,512]{3,0,1,2:T(8,128)(2,1)S(1)} %bitcast.69, bf16[512,1,4,512]{3,0,1,2:T(8,128)(2,1)S(1)} %get-tuple-element.8, bf16[512,1,4,512]{3,0,1,2:T(8,128)(2,1)S(1)} %get-tuple-element.7), kind=kOutput, calls=%fused_computation.13 | convolution fusion | flops 2149580800 | bytes 12582912 | tf_op jit(solution)/shard_map/apct,bpct->cab/dot_general | solution.py:90
  180.9 5.3 %reshape.125 = f32[4,4,128,4,128]{4,3,2,1,0:T(4,128)} reshape(f32[4,512,512]{2,1,0:T(8,128)} %fusion.9) | data formatting | bytes 8388608 | tf_op jit(solution)/shard_map/reshape | solution.py:94
  186.2 4.8 %copy.32 = f32[4,4,128,4,128]{4,2,3,1,0:T(8,128)} copy(f32[4,4,128,4,128]{4,3,2,1,0:T(4,128)} %reshape.125) | data formatting | bytes 8388608 | tf_op jit(solution)/shard_map/reshape | solution.py:94
  191.0 5.3 %reshape.124 = f32[4,4,128,4,128]{4,3,2,1,0:T(4,128)} reshape(f32[4,512,512]{2,1,0:T(8,128)} %convolution_bitcast_fusion) | data formatting | bytes 8388608 | tf_op jit(solution)/shard_map/reshape | solution.py:93
  196.2 4.7 %copy.31 = f32[4,4,128,4,128]{4,2,3,1,0:T(8,128)} copy(f32[4,4,128,4,128]{4,3,2,1,0:T(4,128)} %reshape.124) | data formatting | bytes 8388608 | tf_op jit(solution)/shard_map/reshape | solution.py:93
  201.0 2.9 %gather_fusion.1 = f32[10,4,128,128]{3,2,1,0:T(8,128)S(1)} fusion(f32[4,4,128,4,128]{4,2,3,1,0:T(8,128)} %copy.32, s32[10]{0:T(128)S(1)} %fusion.26), kind=kCustom, calls=%fused_computation.1 | custom fusion | bytes 5242960 | tf_op jit(solution)/shard_map/gather | solution.py:96
  203.9 4.5 %gather_fusion = f32[10,4,128,128]{3,2,1,0:T(8,128)} fusion(f32[4,4,128,4,128]{4,2,3,1,0:T(8,128)} %copy.31, s32[10]{0:T(128)S(1)} %fusion.26), kind=kCustom, calls=%fused_computation | custom fusion | bytes 5242960 | tf_op jit(solution)/shard_map/gather | solution.py:95
  208.4 2.2 maximum_bitcast_fusion
  210.6 0.6 copy.33
  211.2 2.3 %copy-done = f32[4,10,2,128,128]{4,3,2,1,0:T(8,128)} copy-done((f32[4,10,2,128,128]{4,3,2,1,0:T(8,128)}, f32[4,10,2,128,128]{4,3,2,1,0:T(8,128)S(1)}, u32[]{:S(2)}) %copy-start) | copy-done | bytes 5242904
  213.5 1.8 constant_dynamic-slice_fusion
  215.3 0.9 collective-permute-start
  216.2 4.7 %collective-permute-done = f32[20,2,128,128]{3,2,1,0:T(8,128)S(1)} collective-permute-done((f32[20,2,128,128]{3,2,1,0:T(8,128)}, f32[20,2,128,128]{3,2,1,0:T(8,128)S(1)}, u32[]{:S(2)}, u32[]{:S(2)}) %collective-permute-start) | collective-permute-done | bytes 2621472 | tf_op jit(solution)/shard_map/ppermute | solution.py:24
  220.9 3.7 %add_multiply_fusion = f32[20,2,128,128]{3,2,1,0:T(8,128)} fusion(f32[20,2,128,128]{3,2,1,0:T(8,128)S(1)} %collective-permute-done, f32[40,2,128,128]{3,2,1,0:T(8,128)} %bitcast.65, s32[]{:T(128)S(6)} %select_n.76), kind=kLoop, calls=%fused_computation.12 | loop fusion | flops 1310720 | bytes 7864324 | tf_op jit(solution)/shard_map/div | solution.py:108
  (31 shorter events, 1.9 us)
Async XLA Ops:
  36.9 18.2 %copy-start.1 = (s32[32]{0:T(128)S(1)}, s32[32]{0:T(128)}, u32[]{:S(2)}) copy-start(s32[32]{0:T(128)} %param.8) | copy-start | bytes 388
  70.6 6.6 %copy-start.2 = (s32[10]{0:T(128)S(1)}, s32[10]{0:T(128)}, u32[]{:S(2)}) copy-start(s32[10]{0:T(128)} %param.9) | copy-start | bytes 124
  70.7 6.6 %copy-start.3 = (s32[10]{0:T(128)S(1)}, s32[10]{0:T(128)}, u32[]{:S(2)}) copy-start(s32[10]{0:T(128)} %constant.65.clone) | copy-start | bytes 124
  70.7 6.7 %copy-start.4 = (s32[10]{0:T(128)S(1)}, s32[10]{0:T(128)}, u32[]{:S(2)}) copy-start(s32[10]{0:T(128)} %constant.66.clone) | copy-start | bytes 124
  70.7 98.8 %all-to-all-start = ((bf16[16,32,2,4,512]{4,1,3,2,0:T(8,128)(2,1)}), bf16[16,32,2,4,512]{4,1,3,2,0:T(8,128)(2,1)}, u32[]{:S(2)}, u32[]{:S(2)}) async-start(bf16[16,32,2,4,512]{4,1,3,2,0:T(8,128)(2,1)} %bitcast.66), calls=%async_computation | async-start | bytes 8388608 | tf_op jit(solution)/shard_map/all_to_all | solution.py:83
  211.2 2.3 %copy-start = (f32[4,10,2,128,128]{4,3,2,1,0:T(8,128)}, f32[4,10,2,128,128]{4,3,2,1,0:T(8,128)S(1)}, u32[]{:S(2)}) copy-start(f32[4,10,2,128,128]{4,3,2,1,0:T(8,128)S(1)} %copy.33) | copy-start | bytes 15728644
  215.3 5.6 %collective-permute-start = (f32[20,2,128,128]{3,2,1,0:T(8,128)}, f32[20,2,128,128]{3,2,1,0:T(8,128)S(1)}, u32[]{:S(2)}, u32[]{:S(2)}) collective-permute-start(f32[20,2,128,128]{3,2,1,0:T(8,128)} %constant_dynamic-slice_fusion), channel_id=1, source_target_pairs={{0,1},{1,0},{2,3},{3,2},{4,5},{5,4},{6,7},{7,6},{8,9},{9,8},{10,11... | collective-permute-start | bytes 7864328 | tf_op jit(solution)/shard_map/ppermute | solution.py:24
where the time goes:
time: 226 us; the launch traced here: 225 us
  waiting for transfers between devices  96.7 us (43%)
  local copies, waits for them, and re-layouts  59.7 us (26%)
  other arithmetic  40.9 us (18%)
  matrix products  19.5 us (9%)
  starting transfers between devices  7.49 us (3%)
    all_to_all x1, waiting for transfers between devices, on_device(): lax.all_to_all(spectra, 'tile', split_axis=0, concat_axis=1, tiled=True)  92 us
    convert_element_type x1, other arithmetic, weigh(): return summed.astype(jnp.bfloat16)  34.4 us
    reshape x1, local copies, waits for them, and re-layouts, on_device(): frames = weighted.reshape(2, in_dev, tb_count, time_len, NCHAN)  18.2 us
    dot_general x1, matrix products, on_device(): jnp.einsum('rnqoc,ribtn->obiqct', dft_rows, frames, preferred_element_typ...  10.9 us
    reshape x2, local copies, waits for them, and re-layouts, on_device(): imag_full = imag_full.reshape(c_items, NBLK, BLOCK, NBLK, BLOCK)  10.1 us
    reshape x2, local copies, waits for them, and re-layouts, on_device(): real_full = real_full.reshape(c_items, NBLK, BLOCK, NBLK, BLOCK)  10 us
    all_to_all x1, starting transfers between devices, on_device(): lax.all_to_all(spectra, 'tile', split_axis=0, concat_axis=1, tiled=True)  6.63 us
    ppermute x1, waiting for transfers between devices, swapped_2(): return lax.ppermute(block, axis, route)  4.75 us
  transfers between devices with their start and end apart: 2, of which 2 were waited for; matrix products, arithmetic and copies ran while one was open for 0% of the time, Pallas kernels for 0%

commit v1 on v0

--- a/solution.py
+++ b/solution.py
@@ -80,7 +80,10 @@
         "rnqoc,ribtn->obiqct", dft_rows, frames, preferred_element_type=jnp.float32
     )
     spectra = spectra.astype(jnp.bfloat16).reshape(tile_count, in_dev, 2, CH, time_len)
-    received = lax.all_to_all(spectra, "tile", split_axis=0, concat_axis=1, tiled=True)
+    received = jnp.concatenate(
+        lax.all_to_all(jnp.stack(jnp.split(spectra, lax.axis_size("tile"), axis=0)), "tile", 0, 0),
+        axis=1,
+    )
     c_items = received.shape[3]
     flat_inputs = received.reshape(input_total, 2, c_items, time_len)
     swapped = jnp.stack([-flat_inputs[:, 1], flat_inputs[:, 0]], 1)

time: 226 us -> 235 us (1.040)
  local copies, waits for them, and re-layouts: 59.7 us -> 69.3 us
    unnamed x10 -> x25, local copies, waits for them, and re-layouts: 2.31 us -> 13.2 us
where the time goes in v1:
time: 235 us; the launch traced here: 234 us
  waiting for transfers between devices  96.7 us (41%)
  local copies, waits for them, and re-layouts  69.3 us (29%)
  other arithmetic  40.9 us (17%)
  matrix products  19.5 us (8%)
  starting transfers between devices  7.49 us (3%)
    all_to_all x1, waiting for transfers between devices, on_device(): lax.all_to_all(jnp.stack(jnp.split(spectra, lax.axis_size('tile'), axis=0...  92 us
    convert_element_type x1, other arithmetic, weigh(): return summed.astype(jnp.bfloat16)  34.4 us
    reshape x1, local copies, waits for them, and re-layouts, on_device(): frames = weighted.reshape(2, in_dev, tb_count, time_len, NCHAN)  18.2 us
    unnamed x25, local copies, waits for them, and re-layouts  13.2 us
    dot_general x1, matrix products, on_device(): jnp.einsum('rnqoc,ribtn->obiqct', dft_rows, frames, preferred_element_typ...  10.9 us
    reshape x2, local copies, waits for them, and re-layouts, on_device(): imag_full = imag_full.reshape(c_items, NBLK, BLOCK, NBLK, BLOCK)  10.1 us
    reshape x2, local copies, waits for them, and re-layouts, on_device(): real_full = real_full.reshape(c_items, NBLK, BLOCK, NBLK, BLOCK)  10 us
    all_to_all x1, starting transfers between devices, on_device(): lax.all_to_all(jnp.stack(jnp.split(spectra, lax.axis_size('tile'), axis=0...  6.63 us
  transfers between devices with their start and end apart: 2, of which 2 were waited for; matrix products, arithmetic and copies ran while one was open for 0% of the time, Pallas kernels for 0%

profile of v1, /device:TPU:17, one launch (start us, length us, event | category | flops | bytes accessed | tf_op | source)
XLA Modules:
  0.0 234.2 jit_solution(11052370513527778253)
XLA Ops:
  0.0 1.0 slice_bitcast_fusion.23
  2.5 34.4 %add_convert_fusion = bf16[2,32,65536]{2,1,0:T(8,128)(2,1)} fusion(f32[65536]{0:T(1024)S(1)} %mul.182, bf16[2,32,65984]{2,1,0:T(8,128)(2,1)} %param.6, f32[65536]{0:T(1024)S(1)} %mul.179, f32[65536]{0:T(1024)S(1)} %mul.176, f32[65536]{0:T(1024)S(1)} %mul.173, f32[65536]{0:T(1024)S(1)} %mul.170, f32[65536]{0:T(1024)S(1)} %mul.167, f32[65536]{0:T(1024)S(1)} %mul.164, ...), kind=kLoop, calls=%fused_computation.4 | loop fusion | flops 100663296 | bytes 77594624 | tf_op jit(solution)/shard_map/convert_element_type | solution.py:56
  36.9 18.2 %reshape.114 = bf16[2,32,2,512,64]{4,3,2,1,0:T(8,128)(2,1)} reshape(bf16[2,32,65536]{2,1,0:T(8,128)(2,1)} %add_convert_fusion) | data formatting | bytes 16777216 | tf_op jit(solution)/shard_map/reshape | solution.py:78
  55.4 10.9 %fusion.2 = bf16[8,2,32,2,4,512]{5,0,4,3,1,2:T(8,128)(2,1)S(1)} fusion(bf16[1,64,2,8,4]{1,3,0,4,2:T(8,128)(2,1)S(1)} %get-tuple-element.10, bf16[1,64,2,8,4]{1,3,0,4,2:T(8,128)(2,1)S(1)} %get-tuple-element.9, bf16[2,32,2,512,64]{4,3,2,1,0:T(8,128)(2,1)} %reshape.114), kind=kOutput, calls=%fused_computation.7 | convolution fusion | flops 539000832 | bytes 12599296 | tf_op jit(solution)/shard_map/rnqoc,ribtn->obiqct/dot_general | solution.py:79
  66.3 2.4 %copy.44 = bf16[8,2,32,2,4,512]{5,2,4,3,1,0:T(8,128)(2,1)S(1)} copy(bf16[8,2,32,2,4,512]{5,0,4,3,1,2:T(8,128)(2,1)S(1)} %fusion.2) | data formatting | bytes 8388608 | tf_op jit(solution)/shard_map/convert_element_type | solution.py:82
  70.1 0.7 fusion.25
  79.5 0.8 fusion.12
  80.3 6.6 %all-to-all-start = ((bf16[16,1,32,2,4,512]{5,2,4,3,1,0:T(8,128)(2,1)}), bf16[16,1,32,2,4,512]{5,2,4,3,1,0:T(8,128)(2,1)}, u32[]{:S(2)}, u32[]{:S(2)}) async-start(bf16[16,1,32,2,4,512]{5,2,4,3,1,0:T(8,128)(2,1)} %fusion.12), calls=%async_computation | async-start | bytes 8388608 | tf_op jit(solution)/shard_map/all_to_all | solution.py:84
  87.1 92.0 %all-to-all-done = bf16[16,1,32,2,4,512]{5,2,4,3,1,0:T(8,128)(2,1)} async-done(((bf16[16,1,32,2,4,512]{5,2,4,3,1,0:T(8,128)(2,1)}), bf16[16,1,32,2,4,512]{5,2,4,3,1,0:T(8,128)(2,1)}, u32[]{:S(2)}, u32[]{:S(2)}) %all-to-all-start) | async-done | bytes 4194336 | tf_op jit(solution)/shard_map/all_to_all | solution.py:84
  179.1 2.5 %copy.45 = bf16[16,1,32,2,4,512]{5,2,0,3,4,1:T(8,128)(2,1)S(1)} copy(bf16[16,1,32,2,4,512]{5,2,4,3,1,0:T(8,128)(2,1)} %all-to-all-done) | data formatting | bytes 8388608 | tf_op jit(solution)/shard_map/all_to_all | solution.py:84
  181.9 4.3 %convolution_bitcast_fusion = f32[4,512,512]{2,1,0:T(8,128)} fusion(bf16[512,2,4,512]{3,0,1,2:T(8,128)(2,1)S(1)} %bitcast.147), kind=kOutput, calls=%fused_computation.14 | convolution fusion | flops 2147483648 | bytes 8388608 | tf_op jit(solution)/shard_map/apct,bpct->cab/dot_general | solution.py:90
  186.2 4.4 %fusion.9 = f32[4,512,512]{2,1,0:T(8,128)} fusion(bf16[512,2,4,512]{3,0,1,2:T(8,128)(2,1)S(1)} %bitcast.148, bf16[512,1,4,512]{3,0,1,2:T(8,128)(2,1)S(1)} %get-tuple-element.8, bf16[512,1,4,512]{3,0,1,2:T(8,128)(2,1)S(1)} %get-tuple-element.7), kind=kOutput, calls=%fused_computation.13 | convolution fusion | flops 2149580800 | bytes 12582912 | tf_op jit(solution)/shard_map/apct,bpct->cab/dot_general | solution.py:93
  190.5 5.3 %reshape.117 = f32[4,4,128,4,128]{4,3,2,1,0:T(4,128)} reshape(f32[4,512,512]{2,1,0:T(8,128)} %fusion.9) | data formatting | bytes 8388608 | tf_op jit(solution)/shard_map/reshape | solution.py:97
  195.8 4.8 %copy.47 = f32[4,4,128,4,128]{4,2,3,1,0:T(8,128)} copy(f32[4,4,128,4,128]{4,3,2,1,0:T(4,128)} %reshape.117) | data formatting | bytes 8388608 | tf_op jit(solution)/shard_map/reshape | solution.py:97
  200.6 5.3 %reshape.116 = f32[4,4,128,4,128]{4,3,2,1,0:T(4,128)} reshape(f32[4,512,512]{2,1,0:T(8,128)} %convolution_bitcast_fusion) | data formatting | bytes 8388608 | tf_op jit(solution)/shard_map/reshape | solution.py:96
  205.9 4.7 %copy.46 = f32[4,4,128,4,128]{4,2,3,1,0:T(8,128)} copy(f32[4,4,128,4,128]{4,3,2,1,0:T(4,128)} %reshape.116) | data formatting | bytes 8388608 | tf_op jit(solution)/shard_map/reshape | solution.py:96
  210.6 2.9 %gather_fusion.1 = f32[10,4,128,128]{3,2,1,0:T(8,128)S(1)} fusion(f32[4,4,128,4,128]{4,2,3,1,0:T(8,128)} %copy.47, s32[10]{0:T(128)S(1)} %fusion.42), kind=kCustom, calls=%fused_computation.1 | custom fusion | bytes 5242960 | tf_op jit(solution)/shard_map/gather | solution.py:99
  213.5 4.5 %gather_fusion = f32[10,4,128,128]{3,2,1,0:T(8,128)} fusion(f32[4,4,128,4,128]{4,2,3,1,0:T(8,128)} %copy.46, s32[10]{0:T(128)S(1)} %fusion.42), kind=kCustom, calls=%fused_computation | custom fusion | bytes 5242960 | tf_op jit(solution)/shard_map/gather | solution.py:98
  218.0 2.2 maximum_bitcast_fusion
  220.9 2.3 copy-done
  223.1 1.8 constant_dynamic-slice_fusion
  224.9 0.9 collective-permute-start
  225.8 4.7 %collective-permute-done = f32[20,2,128,128]{3,2,1,0:T(8,128)S(1)} collective-permute-done((f32[20,2,128,128]{3,2,1,0:T(8,128)}, f32[20,2,128,128]{3,2,1,0:T(8,128)S(1)}, u32[]{:S(2)}, u32[]{:S(2)}) %collective-permute-start) | collective-permute-done | bytes 2621472 | tf_op jit(solution)/shard_map/ppermute | solution.py:24
  230.5 3.7 %add_multiply_fusion = f32[20,2,128,128]{3,2,1,0:T(8,128)} fusion(f32[20,2,128,128]{3,2,1,0:T(8,128)S(1)} %collective-permute-done, f32[40,2,128,128]{3,2,1,0:T(8,128)} %bitcast.129, s32[]{:T(128)S(6)} %select_n.76), kind=kLoop, calls=%fused_computation.12 | loop fusion | flops 1310720 | bytes 7864324 | tf_op jit(solution)/shard_map/div | solution.py:111
  (47 shorter events, 12.9 us)
Async XLA Ops:
  36.9 18.2 %copy-start.1 = (s32[32]{0:T(128)S(1)}, s32[32]{0:T(128)}, u32[]{:S(2)}) copy-start(s32[32]{0:T(128)} %param.8) | copy-start | bytes 388
  80.3 6.6 %copy-start.2 = (s32[10]{0:T(128)S(1)}, s32[10]{0:T(128)}, u32[]{:S(2)}) copy-start(s32[10]{0:T(128)} %param.9) | copy-start | bytes 124
  80.3 6.6 %copy-start.3 = (s32[10]{0:T(128)S(1)}, s32[10]{0:T(128)}, u32[]{:S(2)}) copy-start(s32[10]{0:T(128)} %constant.65.clone) | copy-start | bytes 124
  80.3 6.7 %copy-start.4 = (s32[10]{0:T(128)S(1)}, s32[10]{0:T(128)}, u32[]{:S(2)}) copy-start(s32[10]{0:T(128)} %constant.66.clone) | copy-start | bytes 124
  80.3 98.8 %all-to-all-start = ((bf16[16,1,32,2,4,512]{5,2,4,3,1,0:T(8,128)(2,1)}), bf16[16,1,32,2,4,512]{5,2,4,3,1,0:T(8,128)(2,1)}, u32[]{:S(2)}, u32[]{:S(2)}) async-start(bf16[16,1,32,2,4,512]{5,2,4,3,1,0:T(8,128)(2,1)} %fusion.12), calls=%async_computation | async-start | bytes 8388608 | tf_op jit(solution)/shard_map/all_to_all | solution.py:84
  220.8 2.3 copy-start
  224.9 5.6 %collective-permute-start = (f32[20,2,128,128]{3,2,1,0:T(8,128)}, f32[20,2,128,128]{3,2,1,0:T(8,128)S(1)}, u32[]{:S(2)}, u32[]{:S(2)}) collective-permute-start(f32[20,2,128,128]{3,2,1,0:T(8,128)} %constant_dynamic-slice_fusion), channel_id=1, source_target_pairs={{0,1},{1,0},{2,3},{3,2},{4,5},{5,4},{6,7},{7,6},{8,9},{9,8},{10,11... | collective-permute-start | bytes 7864328 | tf_op jit(solution)/shard_map/ppermute | solution.py:24
